TPU v7x, 256 devices: a whole 4x4x8 slice. The times are simulated.
256 devices in a mesh: blk: 32 (over x_hi, z, core), tm: 8 (over x_lo, y).
Axes of the slice: x: 4 (x_hi: 2, x_lo: 2; x = x_hi * 2 + x_lo), y: 4, z: 8, core: 2. Of those that a mesh axis runs over, the one named last changes fastest.
Arguments:
- state_base: float32 [8, 5, 512, 32, 128], P('tm', None, 'blk')
- state_now: float32 [8, 5, 512, 32, 128], P('tm', None, 'blk')
- volume: float32 [512, 32, 128], P('blk'), may hold values from 0.5 to 2
- eddy_visc: float32 [512, 32, 128], P('blk'), may hold values from 0.05 to 0.5
- connect: int32 [32, 2, 3], replicated, may hold values from 0 to 31, as said below
- counts: int32 [32], replicated, may hold values from 8 to 16, as said below
Outputs:
- state_next: float32 [8, 5, 512, 32, 128], P('tm', None, 'blk')
Inputs may be any that keep to these rules, and one draw needn't show every extreme that they name: `connect`: blocks form one closed circumferential cycle: the blocks named by a block's two faces are distinct from it; one of them lies exactly half the cycle away in block index, the other within 1 of half the cycle away or, where the cycle closes, next to it; the face, reversal and momentum signs are consistent on both sides of every shared face. `counts`: some block is full and some block is half full.
All inputs are finite; a program needn't handle non-finite values.
Results may differ from a plain program's by a relative error of at most 0.0003.
Values sent between devices are 32-bit elements; how exact they have to be, the bound alone decides.
No kernel may reach another device: no remote copies, remote signals or barrier semaphores. Data moves between devices by JAX's collectives and lax.ppermute only.
A program may use at most 128 MiB of HBM per device.

v0:
```python
import functools

import jax
import jax.numpy as jnp
import numpy as np
from jax import lax
from jax.experimental import pallas as pl
from jax.experimental.pallas import tpu as pltpu
from jax.sharding import PartitionSpec as P

DISS_FOUR = 1.0 / 32.0
NYQUIST = 4.0
F32 = jnp.float32
HBM = pl.BlockSpec(memory_space=pltpu.HBM)
VMEM = pl.BlockSpec(memory_space=pltpu.VMEM)
SMEM = pl.BlockSpec(memory_space=pltpu.SMEM)


def spectral_weights(nt):
    time = np.arange(nt)
    lag = (time[:, None] - time[None, :]) % nt
    parity = 1.0 - 2.0 * (lag % 2)
    angle = np.pi * np.where(lag == 0, 1, lag) / nt
    derivative = np.where(lag == 0, 0.0, -0.5 * parity / np.tan(angle))
    weights = derivative + NYQUIST * parity / nt
    half = nt // 2
    near, far = weights[:half, :half], weights[:half, half:]
    return (0.5 * (near + far)).tolist(), (0.5 * (near - far)).tolist()


def half_side(connect, block, n_blk):
    half = lax.rem(block + n_blk // 2, n_blk)
    return jnp.where(connect[block, 0, 0] == half, 0, 1)


def spectral_kernel(even, odd, got, sent, made, left):
    nt, planes = got.shape[:2]
    half = nt // 2
    gives = [pltpu.make_async_copy(made.at[:, n], sent.at[:, n], left.at[n]) for n in range(planes)]
    for n in range(planes):
        states = [got[b, n] for b in range(nt)]
        sums = [states[b] + states[b + half] for b in range(half)]
        differences = [states[b] - states[b + half] for b in range(half)]
        for a in range(half):
            one = even[a][0] * sums[0]
            two = odd[a][0] * differences[0]
            for b in range(1, half):
                one += even[a][b] * sums[b]
                two += odd[a][b] * differences[b]
            made[a, n] = one + two
            made[a + half, n] = one - two
        gives[n].start()
    for c in gives:
        c.wait()


def final_kernel(kept_hbm, factor_hbm, source_hbm, out_hbm, kept, factor, source, out, arrived, left):
    nv, ni = kept.shape[:2]
    parts = 2
    size = ni // parts
    spots = [(v, pl.ds(h * size, size)) for h in range(parts) for v in range(nv)]
    takes = [
        [
            pltpu.make_async_copy(source_hbm.at[s], source.at[s], arrived.at[0, n]),
            pltpu.make_async_copy(kept_hbm.at[s], kept.at[s], arrived.at[1, n]),
        ]
        for n, s in enumerate(spots)
    ]
    for h in range(parts):
        part = pl.ds(h * size, size)
        takes[h * nv].append(pltpu.make_async_copy(factor_hbm.at[part], factor.at[part], arrived.at[2, h]))
    gives = [pltpu.make_async_copy(out.at[s], out_hbm.at[s], left.at[n]) for n, s in enumerate(spots)]
    for some in takes:
        for c in some:
            c.start()
    for n, s in enumerate(spots):
        for c in takes[n]:
            c.wait()
        out[s] = kept[s] - factor[s[1]] * source[s]
        gives[n].start()
    for c in gives:
        c.wait()


def sensor(before, here, after):
    return jnp.abs(after - 2.0 * here + before) / (after + 2.0 * here + before)


def coefs(nu_a, nu_b, lam_sum, visc_sum):
    e2 = 0.5 * jnp.maximum(nu_a, nu_b)
    e4 = jnp.maximum(0.0, DISS_FOUR - e2)
    lam = 0.5 * lam_sum
    return lam * e2 + 0.5 * visc_sum, lam * e4


def flux(v, d, state, speed, p):
    f = speed * state
    if v == 1 + d:
        f = f + p
    if v == 4:
        f = f + p * speed
    return f


def pressure(state, inv):
    rho, m1, m2, m3, energy = state
    return 0.4 * (energy - 0.5 * (m1 * m1 + m2 * m2 + m3 * m3) * inv)


def section_kernel(
    n_blk, nt, connect, counts, u_hbm, base_hbm, vol_hbm, visc_hbm, kept_hbm, inv_hbm, half_hbm, other_hbm,
    u, base, vol, visc, kept, inv_dens, pkg_half, pkg_other, arrived, left, layer_sems, pkg_sems,
):
    ni, nj, nk = vol.shape
    block = lax.axis_index("blk")
    live = counts[block]
    groups = arrived.shape[1]
    size = ni // groups

    def takes(g):
        part = pl.ds(g * size, size)
        pairs = ((u_hbm, u), (base_hbm, base), (vol_hbm, vol), (visc_hbm, visc))
        return [
            pltpu.make_async_copy(a.at[at], b.at[at], arrived.at[n, g])
            for n, (a, b) in enumerate(pairs)
            for at in [(slice(None), part) if len(a.shape) == 4 else part]
        ]

    def gives(g):
        part = pl.ds(g * size, size)
        return [
            pltpu.make_async_copy(kept.at[:, part], kept_hbm.at[:, part], left.at[0, g]),
            pltpu.make_async_copy(inv_dens.at[part], inv_hbm.at[part], left.at[1, g]),
        ]

    side = half_side(connect, block, n_blk)
    layers = []
    for pkg, face in ((pkg_half, side), (pkg_other, 1 - side)):
        for layer in (0, 1):
            cell = jnp.where(face == 0, layer, live - 1 - layer)
            layers.append(
                pltpu.make_async_copy(u_hbm.at[:, cell], pkg.at[pl.ds(0, 5), layer], layer_sems.at[len(layers)])
            )
            layers.append(pltpu.make_async_copy(visc_hbm.at[cell], pkg.at[5, layer], layer_sems.at[len(layers)]))
    for g in range(groups):
        for c in takes(g):
            c.start()
        if g == 0:
            for c in layers:
                c.start()
    for c in layers:
        c.wait()
    packages = [
        pltpu.make_async_copy(pkg_half, half_hbm, pkg_sems.at[0]),
        pltpu.make_async_copy(pkg_other, other_hbm, pkg_sems.at[1]),
    ]
    for c in packages:
        c.start()

    row = lax.broadcasted_iota(jnp.int32, (nj, nk), 0)
    col = lax.broadcasted_iota(jnp.int32, (nj, nk), 1)
    first_row, last_row = row == 0, row == nj - 1
    first_col, last_col = col == 0, col == nk - 1

    def up_j(x):
        return pltpu.roll(x, nj - 1, 0)

    def down_j(x):
        return pltpu.roll(x, 1, 0)

    def up_k(x):
        return pltpu.roll(x, nk - 1, 1)

    def down_k(x):
        return pltpu.roll(x, 1, 1)

    def plane(i, _):
        inv = 1.0 / u[0, i]
        p = pressure([u[v, i] for v in range(5)], inv)
        c = jnp.sqrt(1.4 * p * inv)
        mu = visc[i]
        speed_j, speed_k = u[2, i] * inv, u[3, i] * inv
        lam_i, lam_j, lam_k = jnp.abs(u[1, i] * inv) + c, jnp.abs(speed_j) + c, jnp.abs(speed_k) + c
        inv_den = 1.0 / (lam_i + lam_j + lam_k + vol[i] * (nt / 2.0))
        inv_dens[i] = inv_den
        nu_j = sensor(jnp.where(first_row, p, down_j(p)), p, jnp.where(last_row, p, up_j(p)))
        c2_j, c4_j = coefs(
            nu_j,
            jnp.where(last_row, nu_j, up_j(nu_j)),
            lam_j + jnp.where(last_row, lam_j, up_j(lam_j)),
            mu + jnp.where(last_row, mu, up_j(mu)),
        )
        nu_k = sensor(jnp.where(first_col, p, down_k(p)), p, jnp.where(last_col, p, up_k(p)))
        c2_k, c4_k = coefs(
            nu_k,
            jnp.where(last_col, 0.0, up_k(nu_k)),
            lam_k + jnp.where(last_col, lam_k, up_k(lam_k)),
            mu + jnp.where(last_col, mu, up_k(mu)),
        )
        wall_k = lam_k * jnp.maximum(0.0, DISS_FOUR - 0.5 * nu_k)
        for v in range(5):
            state = u[v, i]
            mirrored = -state if v == 2 else state
            d1 = jnp.where(last_row, mirrored, up_j(state)) - state
            d2 = d1 - jnp.where(first_row, 2.0 * state if v == 2 else 0.0, down_j(d1))
            d3 = jnp.where(last_row, -d2 if v == 2 else d2, up_j(d2)) - d2
            f = flux(v, 1, state, speed_j, p)
            face = 0.5 * (f + jnp.where(last_row, f if v == 2 else -f, up_j(f))) - c2_j * d1 + c4_j * d3
            wall = 0.0
            if v == 2:
                e2 = 0.5 * nu_j
                wall = f - (lam_j * e2 + mu) * (2.0 * state)
                wall = wall + lam_j * jnp.maximum(0.0, DISS_FOUR - e2) * (2.0 * d1 - 4.0 * state)
            total = face - jnp.where(first_row, wall, down_j(face))
            d1 = jnp.where(last_col, 0.0, up_k(state) - state)
            d2 = d1 - down_k(d1)
            d3 = jnp.where(last_col, 0.0, up_k(d2)) - d2
            f = flux(v, 2, state, speed_k, p)
            face = 0.5 * (f + jnp.where(last_col, f, up_k(f))) - c2_k * d1 + c4_k * d3
            total = total + face - jnp.where(first_col, f + wall_k * d1, down_k(face))
            kept[v, i] = base[v, i] - total * inv_den
        return 0

    def padding(i, _):
        inv_dens[i] = jnp.zeros((nj, nk), F32)
        for v in range(5):
            kept[v, i] = jnp.zeros((nj, nk), F32)
        return 0

    def group(g, _):
        for c in takes(g):
            c.wait()
        start, end = g * size, (g + 1) * size
        middle = jnp.clip(live, start, end)
        lax.fori_loop(start, middle, plane, 0)
        lax.fori_loop(middle, end, padding, 0)
        for c in gives(g):
            c.start()
        return 0

    lax.fori_loop(0, groups, group, 0)
    for g in range(groups):
        for c in gives(g):
            c.wait()
    for c in packages:
        c.wait()


def circumferential_kernel(
    n_blk, connect, counts, u, visc, vol_hbm, kept_hbm, inv_hbm, half_hbm, other_hbm, kept, factor,
    ext, vext, vol, kept_in, inv_dens, got_half, got_other, prs, rho_inv, snd, low, sems,
):
    nv, ni, nj, nk = u.shape
    block = lax.axis_index("blk")
    pairs = [(half_hbm, got_half), (other_hbm, got_other)]
    pairs += [(u.at[v], ext.at[v, pl.ds(2, ni)]) for v in range(nv)]
    pairs += [(visc, vext.at[pl.ds(2, ni)])]
    late = [(inv_hbm, inv_dens), (vol_hbm, vol)] + [(kept_hbm.at[v], kept_in.at[v]) for v in range(nv)]
    copies = [pltpu.make_async_copy(*pair, sems.at[n]) for n, pair in enumerate(pairs + late)]
    for c in copies:
        c.start()
    for c in copies[: len(pairs)]:
        c.wait()
    live = counts[block]
    side_of_half = half_side(connect, block, n_blk)
    turned = (nk - 1) - lax.broadcasted_iota(jnp.int32, (nj, nk), 1)

    def place(side, got):
        facing, reversal = connect[block, side, 1], connect[block, side, 2]
        sign_i = jnp.where(facing == side, -1.0, 1.0)
        sign_k = jnp.where(reversal == 1, -1.0, 1.0)

        def write(turn):
            for layer in (0, 1):
                at = 1 - layer if side == 0 else live + 2 + layer
                for v in range(6):
                    plane = got[v, layer]
                    if turn:
                        plane = jnp.take_along_axis(plane, turned, axis=1, mode="promise_in_bounds")
                    if v == 1:
                        plane = plane * sign_i
                    if v == 3:
                        plane = plane * sign_k
                    if v < 5:
                        ext[v, at] = plane
                    else:
                        vext[at] = plane

        pl.when(reversal == 1)(lambda: write(True))
        pl.when(reversal != 1)(lambda: write(False))

    @pl.when(side_of_half == 0)
    def _():
        place(0, got_half)
        place(1, got_other)

    @pl.when(side_of_half != 0)
    def _():
        place(1, got_half)
        place(0, got_other)

    def primitives(e, _):
        inv = 1.0 / ext[0, e]
        p = pressure([ext[v, e] for v in range(5)], inv)
        rho_inv[e] = inv
        prs[e] = p
        snd[e] = jnp.sqrt(1.4 * p * inv)
        return 0

    lax.fori_loop(0, live + 4, primitives, 0)

    def circ_face(e):
        p0, p1, p2, p3 = (prs[e + k] for k in (-1, 0, 1, 2))
        s1, s2 = ext[1, e] * rho_inv[e], ext[1, e + 1] * rho_inv[e + 1]
        lam_sum = (jnp.abs(s1) + snd[e]) + (jnp.abs(s2) + snd[e + 1])
        c2, c4 = coefs(sensor(p0, p1, p2), sensor(p1, p2, p3), lam_sum, vext[e] + vext[e + 1])
        for v in range(5):
            u0, u1, u2, u3 = (ext[v, e + k] for k in (-1, 0, 1, 2))
            d1 = u2 - u1
            d3 = (u3 - u2) - 2.0 * d1 + (u1 - u0)
            yield 0.5 * (flux(v, 0, u1, s1, p1) + flux(v, 0, u2, s2, p2)) - c2 * d1 + c4 * d3

    for v, f in enumerate(circ_face(1)):
        low[v] = f
    for c in copies[len(pairs) :]:
        c.wait()

    def plane(i, _):
        inv_den = inv_dens[i]
        factor[i] = vol[i] * inv_den
        for v, f in enumerate(circ_face(i + 2)):
            kept[v, i] = kept_in[v, i] - (f - low[v]) * inv_den
            low[v] = f
        return 0

    lax.fori_loop(0, live, plane, 0)

    def padding(i, _):
        factor[i] = jnp.zeros((nj, nk), F32)
        for v in range(5):
            kept[v, i] = jnp.zeros((nj, nk), F32)
        return 0

    lax.fori_loop(live, ni, padding, 0)


def local(n_blk, nt, state_base, state_now, volume, eddy_visc, connect, counts):
    u, base = state_now[0], state_base[0]
    nv, ni, nj, nk = u.shape
    state = jax.ShapeDtypeStruct(u.shape, F32)
    cells = jax.ShapeDtypeStruct(volume.shape, F32)
    package = jax.ShapeDtypeStruct((nv + 1, 2, nj, nk), F32)

    def vmem(x):
        return pltpu.VMEM(x.shape, x.dtype)


    got = lax.all_to_all(u.reshape(nt, nv * ni // nt, nj, nk), "tm", 0, 0, tiled=True)

    groups = 4
    kept, inv_dens, pkg_half, pkg_other = pl.pallas_call(
        functools.partial(section_kernel, n_blk, nt),
        out_shape=[state, cells, package, package],
        in_specs=[SMEM, SMEM] + [HBM] * 4,
        out_specs=[HBM] * 4,
        scratch_shapes=[vmem(x) for x in (state, state, cells, cells, state, cells, package, package)]
        + [pltpu.SemaphoreType.DMA(n) for n in ((4, groups), (2, groups), (8,), (2,))],
        compiler_params=pltpu.CompilerParams(vmem_limit_bytes=62 * 2**20),
        cost_estimate=pl.CostEstimate(flops=400 * u.size, bytes_accessed=16 * u.size, transcendentals=6 * volume.size),
        name="section",
    )(connect, counts, u, base, volume, eddy_visc)

    got, _ = lax.optimization_barrier((got, kept))

    half = n_blk // 2
    got_half = lax.ppermute(pkg_half, "blk", [(b, (b + half) % n_blk) for b in range(n_blk)])
    others = [(n_blk - 1 - b) if b in (0, n_blk - 1) else (b + half - 1) if b < half else (b - half + 1) for b in range(n_blk)]
    got_other = lax.ppermute(pkg_other, "blk", list(enumerate(others)))
    ids = jnp.arange(n_blk, dtype=jnp.int32)
    rest = jnp.where(
        (ids == 0) | (ids == n_blk - 1), n_blk - 1 - ids, jnp.where(ids < half, ids + half - 1, ids - half + 1)
    )
    halves = lax.rem(ids + half, n_blk)
    names = connect[:, :, 0]
    usual = jnp.all(
        ((names[:, 0] == halves) & (names[:, 1] == rest)) | ((names[:, 1] == halves) & (names[:, 0] == rest))
    )

    def by_ring(pkg, got_it):
        block = lax.axis_index("blk")
        there = connect[block, 1 - half_side(connect, block, n_blk), 0]

        def step(n, carry):
            moving, found = carry
            moving = lax.ppermute(moving, "blk", [(b, (b + 1) % n_blk) for b in range(n_blk)])
            return moving, jnp.where(lax.rem(block - n + n_blk, n_blk) == there, moving, found)

        return lax.fori_loop(1, n_blk, step, (pkg, got_it))[1]

    sent = pl.pallas_call(
        functools.partial(spectral_kernel, *spectral_weights(nt)),
        out_shape=jax.ShapeDtypeStruct(got.shape, F32),
        in_specs=[VMEM],
        out_specs=HBM,
        scratch_shapes=[vmem(got), pltpu.SemaphoreType.DMA((got.shape[1],))],
        compiler_params=pltpu.CompilerParams(vmem_limit_bytes=8 * 2**20),
        cost_estimate=pl.CostEstimate(flops=2 * nt * u.size, bytes_accessed=8 * u.size, transcendentals=0),
        name="spectral",
    )(got)
    got_half, got_other, _ = lax.optimization_barrier((got_half, got_other, sent))
    got_other = lax.cond(usual, lambda pkg, got_it: got_it, by_ring, pkg_other, got_other)
    source = lax.all_to_all(sent, "tm", 0, 0, tiled=True)

    ghosted = jax.ShapeDtypeStruct((ni + 4, nj, nk), F32)
    kept, factor = pl.pallas_call(
        functools.partial(circumferential_kernel, n_blk),
        out_shape=[state, cells],
        in_specs=[SMEM, SMEM] + [HBM] * 7,
        out_specs=[VMEM, VMEM],
        scratch_shapes=[pltpu.VMEM((nv,) + ghosted.shape, F32)]
        + [vmem(x) for x in (ghosted, cells, state, cells, package, package, ghosted, ghosted, ghosted)]
        + [pltpu.VMEM((nv, nj, nk), F32), pltpu.SemaphoreType.DMA((2 * nv + 5,))],
        compiler_params=pltpu.CompilerParams(vmem_limit_bytes=64 * 2**20),
        cost_estimate=pl.CostEstimate(flops=200000 * u.size, bytes_accessed=12 * u.size, transcendentals=2 * volume.size),
        name="circumferential",
    )(connect, counts, u, eddy_visc, volume, kept, inv_dens, got_half, got_other)

    out = pl.pallas_call(
        final_kernel,
        out_shape=state,
        in_specs=[HBM] * 3,
        out_specs=HBM,
        scratch_shapes=[vmem(x) for x in (state, cells, state, state)]
        + [pltpu.SemaphoreType.DMA(n) for n in ((3, 2 * nv), (2 * nv,))],
        compiler_params=pltpu.CompilerParams(vmem_limit_bytes=64 * 2**20),
        name="final",
    )(kept, factor, source.reshape(u.shape))
    return out[None]


def solution(mesh):
    n_blk, nt = mesh.shape["blk"], mesh.shape["tm"]
    state, cells = P("tm", None, "blk", None, None), P("blk", None, None)
    return jax.shard_map(
        functools.partial(local, n_blk, nt),
        mesh=mesh,
        in_specs=(state, state, cells, cells, P(), P()),
        out_specs=state,
        check_vma=False,
    )
```

profile of v0, /device:TPU:102, one launch (start us, length us, event | category | flops | bytes accessed | tf_op | source)
XLA Modules:
  0.0 49.8 jit_solution(15885582198765834117)
XLA Ops:
  0.0 0.0 copy-start
  0.0 6.1 %all-to-all-start = ((f32[8,10,32,128]{3,2,1,0:T(8,128)}), f32[8,10,32,128]{3,2,1,0:T(8,128)S(1)}, u32[]{:S(2)}, u32[]{:S(2)}) async-start(f32[8,10,32,128]{3,2,1,0:T(8,128)} %bitcast.13), calls=%async_computation | async-start | bytes 2621440 | tf_op jit(solution)/shard_map/all_to_all | solution.py:358
  6.1 0.0 copy-done
  6.1 0.7 %copy.8.connect = s32[32,2,3]{2,1,0:T(2,128)} copy(s32[32,2,3]{0,1,2:T(2,128)S(1)} %copy-done) | data formatting | bytes 1536 | tf_op args[4]
  6.8 7.6 %section.1 = (f32[5,16,32,128]{3,2,1,0:T(8,128)}, f32[16,32,128]{2,1,0:T(8,128)}, f32[6,2,32,128]{3,2,1,0:T(8,128)}, f32[6,2,32,128]{3,2,1,0:T(8,128)S(1)}) custom-call(s32[32,2,3]{2,1,0:T(2,128)} %copy.8.connect, s32[32]{0:T(128)} %counts.3, f32[5,16,32,128]{3,2,1,0:T(8,128)} %bitcast.14, f32[5,16,32,128]{3,2,1,0:T(8,128)} %bitcast.16, ...), custom_call_target="tpu_custom_call" | custom-call | flops 131072000 | bytes 5242880 | tf_op jit(solution)/shard_map/section/pallas_call | solution.py:361
  14.4 2.3 %collective-permute-start.1 = (f32[6,2,32,128]{3,2,1,0:T(8,128)}, f32[6,2,32,128]{3,2,1,0:T(8,128)S(1)}, u32[]{:S(2)}, u32[]{:S(2)}) collective-permute-start(f32[6,2,32,128]{3,2,1,0:T(8,128)} %get-tuple-element.123), channel_id=1, source_target_pairs={{0,128},{8,136},{16,144},{24,152},{32,160},{40,168},{48,176},{56,1... | collective-permute-start | bytes 589832 | tf_op jit(solution)/shard_map/ppermute | solution.py:376
  16.7 0.0 collective-permute-start.2
  16.7 0.7 %or_reduce_fusion = pred[]{:T(512)} fusion(s32[32,2]{0,1:T(2,128)S(1)} %slice_bitcast_fusion), kind=kLoop, calls=%fused_computation.5 | loop fusion | flops 767 | bytes 257 | tf_op jit(solution)/shard_map/reduce_and | solution.py:385
  18.1 6.0 %all-to-all-done.got = f32[8,10,32,128]{3,2,1,0:T(8,128)S(1)} async-done(((f32[8,10,32,128]{3,2,1,0:T(8,128)}), f32[8,10,32,128]{3,2,1,0:T(8,128)S(1)}, u32[]{:S(2)}, u32[]{:S(2)}) %all-to-all-start) | async-done | bytes 1310752 | tf_op jit(solution)/shard_map/all_to_all | solution.py:358
  24.1 1.2 %spectral.1 = f32[8,10,32,128]{3,2,1,0:T(8,128)} custom-call(f32[8,10,32,128]{3,2,1,0:T(8,128)S(1)} %all-to-all-done.got), custom_call_target="tpu_custom_call" | custom-call | flops 5242880 | bytes 2621440 | tf_op jit(solution)/shard_map/spectral/pallas_call | solution.py:400
  25.3 6.3 %all-to-all-start.1 = ((f32[8,10,32,128]{3,2,1,0:T(8,128)}), f32[8,10,32,128]{3,2,1,0:T(8,128)}, u32[]{:S(2)}, u32[]{:S(2)}) async-start(f32[8,10,32,128]{3,2,1,0:T(8,128)} %spectral.1), calls=%async_computation.1 | async-start | bytes 2621440 | tf_op jit(solution)/shard_map/all_to_all | solution.py:412
  31.6 0.0 collective-permute-done.1.half_hbm
  31.6 0.0 copy-start.1
  31.6 0.0 collective-permute-done.2
  31.6 0.7 %copy-done.1 = f32[6,2,32,128]{3,2,1,0:T(8,128)} copy-done((f32[6,2,32,128]{3,2,1,0:T(8,128)}, f32[6,2,32,128]{3,2,1,0:T(8,128)S(1)}, u32[]{:S(2)}) %copy-start.1) | copy-done | bytes 196632
  32.3 5.4 %circumferential.1 = (f32[5,16,32,128]{3,2,1,0:T(8,128)}, f32[16,32,128]{2,1,0:T(8,128)}) custom-call(s32[32,2,3]{2,1,0:T(2,128)} %copy.8.connect, s32[32]{0:T(128)} %counts.3, f32[5,16,32,128]{3,2,1,0:T(8,128)} %bitcast.15, f32[16,32,128]{2,1,0:T(8,128)} %visc.1, f32[16,32,128]{2,1,0:T(8,128)} %vol_hbm.3, f32[5,16,32,128]{3,2,1,0:T(8,128)} %get-tuple-element.121.kept_hbm, ...), custom_call_target="tpu_custom_call" | custom-call | flops 65536000000 | bytes 3932160 | tf_op jit(solution)/shard_map/circumferential/pallas_call | solution.py:415
  37.6 9.3 %all-to-all-done.1 = f32[8,10,32,128]{3,2,1,0:T(8,128)} async-done(((f32[8,10,32,128]{3,2,1,0:T(8,128)}), f32[8,10,32,128]{3,2,1,0:T(8,128)}, u32[]{:S(2)}, u32[]{:S(2)}) %all-to-all-start.1) | async-done | bytes 1310752 | tf_op jit(solution)/shard_map/all_to_all | solution.py:412
  46.9 2.9 %final.1 = f32[5,16,32,128]{3,2,1,0:T(8,128)} custom-call(f32[5,16,32,128]{3,2,1,0:T(8,128)} %get-tuple-element.128.kept_hbm, f32[16,32,128]{2,1,0:T(8,128)} %get-tuple-element.129.factor_hbm, f32[5,16,32,128]{3,2,1,0:T(8,128)} %bitcast.8.source_hbm), custom_call_target="tpu_custom_call" | custom-call | tf_op jit(solution)/shard_map/final/pallas_call | solution.py:428
  (2 shorter events, 0.0 us)
Async XLA Ops:
  0.0 6.1 %copy-start = (s32[32,2,3]{0,1,2:T(2,128)S(1)}, s32[32,2,3]{0,1,2:T(2,128)}, u32[]{:S(2)}) copy-start(s32[32,2,3]{0,1,2:T(2,128)} %param.14) | copy-start | bytes 2308
  0.0 24.1 %all-to-all-start = ((f32[8,10,32,128]{3,2,1,0:T(8,128)}), f32[8,10,32,128]{3,2,1,0:T(8,128)S(1)}, u32[]{:S(2)}, u32[]{:S(2)}) async-start(f32[8,10,32,128]{3,2,1,0:T(8,128)} %bitcast.13), calls=%async_computation | async-start | bytes 2621440 | tf_op jit(solution)/shard_map/all_to_all | solution.py:358
  14.4 17.2 %collective-permute-start.1 = (f32[6,2,32,128]{3,2,1,0:T(8,128)}, f32[6,2,32,128]{3,2,1,0:T(8,128)S(1)}, u32[]{:S(2)}, u32[]{:S(2)}) collective-permute-start(f32[6,2,32,128]{3,2,1,0:T(8,128)} %get-tuple-element.123), channel_id=1, source_target_pairs={{0,128},{8,136},{16,144},{24,152},{32,160},{40,168},{48,176},{56,1... | collective-permute-start | bytes 589832 | tf_op jit(solution)/shard_map/ppermute | solution.py:376
  16.7 14.9 %collective-permute-start.2 = (f32[6,2,32,128]{3,2,1,0:T(8,128)S(1)}, f32[6,2,32,128]{3,2,1,0:T(8,128)}, u32[]{:S(2)}, u32[]{:S(2)}) collective-permute-start(f32[6,2,32,128]{3,2,1,0:T(8,128)S(1)} %get-tuple-element.124), channel_id=1, source_target_pairs={{0,248},{8,128},{16,136},{24,144},{32,152},{40,160},{48,168},{56,1... | collective-permute-start | bytes 589832 | tf_op jit(solution)/shard_map/ppermute | solution.py:378
  25.3 21.7 %all-to-all-start.1 = ((f32[8,10,32,128]{3,2,1,0:T(8,128)}), f32[8,10,32,128]{3,2,1,0:T(8,128)}, u32[]{:S(2)}, u32[]{:S(2)}) async-start(f32[8,10,32,128]{3,2,1,0:T(8,128)} %spectral.1), calls=%async_computation.1 | async-start | bytes 2621440 | tf_op jit(solution)/shard_map/all_to_all | solution.py:412
  31.6 0.7 %copy-start.1 = (f32[6,2,32,128]{3,2,1,0:T(8,128)}, f32[6,2,32,128]{3,2,1,0:T(8,128)S(1)}, u32[]{:S(2)}) copy-start(f32[6,2,32,128]{3,2,1,0:T(8,128)S(1)} %collective-permute-done.1.half_hbm) | copy-start | bytes 589828
where the time goes:
time: 50.7 us; the launch traced here: 49.8 us
  Pallas kernels  17 us (34%)
  waiting for transfers between devices  15.3 us (30%)
  starting transfers between devices  14.7 us (29%)
  local copies, waits for them, and re-layouts  1.38 us (3%)
  between operations  0.72 us (1%)
  other arithmetic  0.71 us (1%)
    all_to_all x1, waiting for transfers between devices, local(): source = lax.all_to_all(sent, 'tm', 0, 0, tiled=True)  9.29 us
    pallas_call x1, Pallas kernels, local(): pl.pallas_call(functools.partial(section_kernel, n_blk, nt), out_shape=[s...  7.62 us
    all_to_all x1, starting transfers between devices, local(): source = lax.all_to_all(sent, 'tm', 0, 0, tiled=True)  6.31 us
    all_to_all x1, starting transfers between devices, local(): lax.all_to_all(u.reshape(nt, nv * ni // nt, nj, nk), 'tm', 0, 0, tiled=True)  6.06 us
    all_to_all x1, waiting for transfers between devices, local(): lax.all_to_all(u.reshape(nt, nv * ni // nt, nj, nk), 'tm', 0, 0, tiled=True)  5.97 us
    pallas_call x1, Pallas kernels, local(): pl.pallas_call(functools.partial(circumferential_kernel, n_blk), out_shap...  5.36 us
    pallas_call x1, Pallas kernels, local(): pl.pallas_call(final_kernel, out_shape=state, in_specs=[HBM] * 3, out_spe...  2.86 us
    ppermute x1, starting transfers between devices, local(): lax.ppermute(pkg_half, 'blk', [(b, (b + half) % n_blk) for b in range(n_b...  2.32 us
  transfers between devices with their start and end apart: 4, of which 2 were waited for; matrix products, arithmetic and copies ran while one was open for 3% of the time, Pallas kernels for 28%

commit v1 on v0

--- a/solution.py
+++ b/solution.py
@@ -36,7 +36,10 @@
 def spectral_kernel(even, odd, got, sent, made, left):
     nt, planes = got.shape[:2]
     half = nt // 2
-    gives = [pltpu.make_async_copy(made.at[:, n], sent.at[:, n], left.at[n]) for n in range(planes)]
+    groups = left.shape[0]
+    size = planes // groups
+    parts = [pl.ds(g * size, size) for g in range(groups)]
+    gives = [pltpu.make_async_copy(made.at[:, part], sent.at[:, part], left.at[g]) for g, part in enumerate(parts)]
     for n in range(planes):
         states = [got[b, n] for b in range(nt)]
         sums = [states[b] + states[b + half] for b in range(half)]
@@ -49,37 +52,28 @@
                 two += odd[a][b] * differences[b]
             made[a, n] = one + two
             made[a + half, n] = one - two
-        gives[n].start()
+        if n % size == size - 1:
+            gives[n // size].start()
     for c in gives:
         c.wait()
 
 
-def final_kernel(kept_hbm, factor_hbm, source_hbm, out_hbm, kept, factor, source, out, arrived, left):
-    nv, ni = kept.shape[:2]
-    parts = 2
-    size = ni // parts
-    spots = [(v, pl.ds(h * size, size)) for h in range(parts) for v in range(nv)]
-    takes = [
-        [
-            pltpu.make_async_copy(source_hbm.at[s], source.at[s], arrived.at[0, n]),
-            pltpu.make_async_copy(kept_hbm.at[s], kept.at[s], arrived.at[1, n]),
-        ]
-        for n, s in enumerate(spots)
-    ]
-    for h in range(parts):
-        part = pl.ds(h * size, size)
-        takes[h * nv].append(pltpu.make_async_copy(factor_hbm.at[part], factor.at[part], arrived.at[2, h]))
-    gives = [pltpu.make_async_copy(out.at[s], out_hbm.at[s], left.at[n]) for n, s in enumerate(spots)]
-    for some in takes:
-        for c in some:
-            c.start()
-    for n, s in enumerate(spots):
-        for c in takes[n]:
-            c.wait()
-        out[s] = kept[s] - factor[s[1]] * source[s]
-        gives[n].start()
+def final_kernel(kept, factor, source_hbm, out_hbm, source, out, arrived, left):
+    nv = kept.shape[0]
+    takes = [pltpu.make_async_copy(source_hbm.at[v], source.at[v], arrived.at[v]) for v in range(nv)]
+    gives = [pltpu.make_async_copy(out.at[v], out_hbm.at[v], left.at[v]) for v in range(nv)]
+    for c in takes:
+        c.start()
+    for v in range(nv):
+        takes[v].wait()
+        out[v] = kept[v] - factor[...] * source[v]
+        gives[v].start()
     for c in gives:
         c.wait()
+
+
+def factor_kernel(vol, inv_dens, factor):
+    factor[...] = vol[...] * inv_dens[...]
 
 
 def sensor(before, here, after):
@@ -247,15 +241,15 @@
 
 
 def circumferential_kernel(
-    n_blk, connect, counts, u, visc, vol_hbm, kept_hbm, inv_hbm, half_hbm, other_hbm, kept, factor,
-    ext, vext, vol, kept_in, inv_dens, got_half, got_other, prs, rho_inv, snd, low, sems,
+    n_blk, connect, counts, u, visc, kept_hbm, inv_hbm, half_hbm, other_hbm, kept,
+    ext, vext, kept_in, inv_dens, got_half, got_other, prs, rho_inv, snd, low, sems,
 ):
     nv, ni, nj, nk = u.shape
     block = lax.axis_index("blk")
     pairs = [(half_hbm, got_half), (other_hbm, got_other)]
     pairs += [(u.at[v], ext.at[v, pl.ds(2, ni)]) for v in range(nv)]
     pairs += [(visc, vext.at[pl.ds(2, ni)])]
-    late = [(inv_hbm, inv_dens), (vol_hbm, vol)] + [(kept_hbm.at[v], kept_in.at[v]) for v in range(nv)]
+    late = [(inv_hbm, inv_dens)] + [(kept_hbm.at[v], kept_in.at[v]) for v in range(nv)]
     copies = [pltpu.make_async_copy(*pair, sems.at[n]) for n, pair in enumerate(pairs + late)]
     for c in copies:
         c.start()
@@ -327,7 +321,6 @@
 
     def plane(i, _):
         inv_den = inv_dens[i]
-        factor[i] = vol[i] * inv_den
         for v, f in enumerate(circ_face(i + 2)):
             kept[v, i] = kept_in[v, i] - (f - low[v]) * inv_den
             low[v] = f
@@ -336,7 +329,6 @@
     lax.fori_loop(0, live, plane, 0)
 
     def padding(i, _):
-        factor[i] = jnp.zeros((nj, nk), F32)
         for v in range(5):
             kept[v, i] = jnp.zeros((nj, nk), F32)
         return 0
@@ -402,7 +394,7 @@
         out_shape=jax.ShapeDtypeStruct(got.shape, F32),
         in_specs=[VMEM],
         out_specs=HBM,
-        scratch_shapes=[vmem(got), pltpu.SemaphoreType.DMA((got.shape[1],))],
+        scratch_shapes=[vmem(got), pltpu.SemaphoreType.DMA((nv,))],
         compiler_params=pltpu.CompilerParams(vmem_limit_bytes=8 * 2**20),
         cost_estimate=pl.CostEstimate(flops=2 * nt * u.size, bytes_accessed=8 * u.size, transcendentals=0),
         name="spectral",
@@ -411,28 +403,37 @@
     got_other = lax.cond(usual, lambda pkg, got_it: got_it, by_ring, pkg_other, got_other)
     source = lax.all_to_all(sent, "tm", 0, 0, tiled=True)
 
+    factor = pl.pallas_call(
+        factor_kernel,
+        out_shape=cells,
+        in_specs=[VMEM] * 2,
+        out_specs=VMEM,
+        compiler_params=pltpu.CompilerParams(vmem_limit_bytes=64 * 2**20),
+        name="factor",
+    )(volume, lax.optimization_barrier((inv_dens, sent))[0])
+    kept, factor = lax.optimization_barrier((kept, factor))
+
     ghosted = jax.ShapeDtypeStruct((ni + 4, nj, nk), F32)
-    kept, factor = pl.pallas_call(
+    kept = pl.pallas_call(
         functools.partial(circumferential_kernel, n_blk),
-        out_shape=[state, cells],
-        in_specs=[SMEM, SMEM] + [HBM] * 7,
-        out_specs=[VMEM, VMEM],
+        out_shape=state,
+        in_specs=[SMEM, SMEM] + [HBM] * 6,
+        out_specs=VMEM,
         scratch_shapes=[pltpu.VMEM((nv,) + ghosted.shape, F32)]
-        + [vmem(x) for x in (ghosted, cells, state, cells, package, package, ghosted, ghosted, ghosted)]
-        + [pltpu.VMEM((nv, nj, nk), F32), pltpu.SemaphoreType.DMA((2 * nv + 5,))],
-        compiler_params=pltpu.CompilerParams(vmem_limit_bytes=64 * 2**20),
+        + [vmem(x) for x in (ghosted, state, cells, package, package, ghosted, ghosted, ghosted)]
+        + [pltpu.VMEM((nv, nj, nk), F32), pltpu.SemaphoreType.DMA((2 * nv + 4,))],
+        compiler_params=pltpu.CompilerParams(vmem_limit_bytes=40 * 2**20),
         cost_estimate=pl.CostEstimate(flops=200000 * u.size, bytes_accessed=12 * u.size, transcendentals=2 * volume.size),
         name="circumferential",
-    )(connect, counts, u, eddy_visc, volume, kept, inv_dens, got_half, got_other)
+    )(connect, counts, u, eddy_visc, kept, inv_dens, got_half, got_other)
 
     out = pl.pallas_call(
         final_kernel,
         out_shape=state,
-        in_specs=[HBM] * 3,
+        in_specs=[VMEM, VMEM, HBM],
         out_specs=HBM,
-        scratch_shapes=[vmem(x) for x in (state, cells, state, state)]
-        + [pltpu.SemaphoreType.DMA(n) for n in ((3, 2 * nv), (2 * nv,))],
-        compiler_params=pltpu.CompilerParams(vmem_limit_bytes=64 * 2**20),
+        scratch_shapes=[vmem(state)] * 2 + [pltpu.SemaphoreType.DMA((nv,))] * 2,
+        compiler_params=pltpu.CompilerParams(vmem_limit_bytes=8 * 2**20),
         name="final",
     )(kept, factor, source.reshape(u.shape))
     return out[None]

time: 50.7 us -> 49.7 us (0.980); the launches traced: 49.8 us -> 49.4 us
  local copies, waits for them, and re-layouts: 1.38 us -> 5.08 us
  waiting for transfers between devices: 15.3 us -> 12.4 us
  Pallas kernels: 17 us -> 16 us
    unnamed x5 -> x23, local copies, waits for them, and re-layouts: 1.37 us -> 5.08 us
    all_to_all x1, waiting for transfers between devices: 9.29 us -> 5.91 us  [local(): source = lax.all_to_all(sent, 'tm', 0, 0, tiled=True)]
    pallas_call x1, Pallas kernels: 5.36 us -> 3.61 us  [local(): pl.pallas_call(functools.partial(circumferential_kernel, n_blk), out_shap...]
    pallas_call x1 -> x2, Pallas kernels: 2.86 us -> 3.87 us  [the longest x1 2.12 us: local(): pl.pallas_call(final_kernel, out_shape=state, in_specs=[VMEM, VMEM, HBM],...]
    all_to_all x1, waiting for transfers between devices: 5.97 us -> 6.54 us  [local(): lax.all_to_all(u.reshape(nt, nv * ni // nt, nj, nk), 'tm', 0, 0, tiled=True)]
where the time goes in v1:
time: 49.7 us; the launch traced here: 49.4 us
  Pallas kernels  16 us (32%)
  starting transfers between devices  14.6 us (29%)
  waiting for transfers between devices  12.4 us (25%)
  local copies, waits for them, and re-layouts  5.08 us (10%)
  other arithmetic  0.64 us (1%)
  between operations  0.64 us (1%)
    pallas_call x1, Pallas kernels, local(): pl.pallas_call(functools.partial(section_kernel, n_blk, nt), out_shape=[s...  7.32 us
    all_to_all x1, waiting for transfers between devices, local(): lax.all_to_all(u.reshape(nt, nv * ni // nt, nj, nk), 'tm', 0, 0, tiled=True)  6.54 us
    all_to_all x1, starting transfers between devices, local(): source = lax.all_to_all(sent, 'tm', 0, 0, tiled=True)  6.31 us
    all_to_all x1, starting transfers between devices, local(): lax.all_to_all(u.reshape(nt, nv * ni // nt, nj, nk), 'tm', 0, 0, tiled=True)  6.06 us
    all_to_all x1, waiting for transfers between devices, local(): source = lax.all_to_all(sent, 'tm', 0, 0, tiled=True)  5.91 us
    unnamed x23, local copies, waits for them, and re-layouts  5.08 us
    pallas_call x1, Pallas kernels, local(): pl.pallas_call(functools.partial(circumferential_kernel, n_blk), out_shap...  3.61 us
    pallas_call x1, Pallas kernels, local(): pl.pallas_call(final_kernel, out_shape=state, in_specs=[VMEM, VMEM, HBM],...  2.12 us
  transfers between devices with their start and end apart: 4, of which 2 were waited for; matrix products, arithmetic and copies ran while one was open for 3% of the time, Pallas kernels for 28%

profile of v1, /device:TPU:102, one launch (start us, length us, event | category | flops | bytes accessed | tf_op | source)
XLA Modules:
  0.0 49.4 jit_solution(6541337099734928856)
XLA Ops:
  0.0 0.0 copy-start.9
  0.0 6.1 %all-to-all-start = ((f32[8,10,32,128]{3,2,1,0:T(8,128)}), f32[8,10,32,128]{3,2,1,0:T(8,128)S(1)}, u32[]{:S(2)}, u32[]{:S(2)}) async-start(f32[8,10,32,128]{3,2,1,0:T(8,128)} %bitcast.13), calls=%async_computation | async-start | bytes 2621440 | tf_op jit(solution)/shard_map/all_to_all | solution.py:350
  6.1 0.0 copy-done.9
  6.1 0.7 %copy.8.connect = s32[32,2,3]{2,1,0:T(2,128)} copy(s32[32,2,3]{0,1,2:T(2,128)S(1)} %copy-done.9) | data formatting | bytes 1536 | tf_op args[4]
  6.8 7.3 %section.1 = (f32[5,16,32,128]{3,2,1,0:T(8,128)}, f32[16,32,128]{2,1,0:T(8,128)}, f32[6,2,32,128]{3,2,1,0:T(8,128)}, f32[6,2,32,128]{3,2,1,0:T(8,128)S(1)}) custom-call(s32[32,2,3]{2,1,0:T(2,128)} %copy.8.connect, s32[32]{0:T(128)} %counts.3, f32[5,16,32,128]{3,2,1,0:T(8,128)} %bitcast.14, f32[5,16,32,128]{3,2,1,0:T(8,128)} %bitcast.16, f32[16,32,128]{2,1,0:T(8,128)} %vol.1, ...), custom_call_target="tpu_custom_call" | custom-call | flops 131072000 | bytes 5242880 | tf_op jit(solution)/shard_map/section/pallas_call | solution.py:353
  14.1 0.0 copy-start.10
  14.1 2.1 %collective-permute-start.1 = (f32[6,2,32,128]{3,2,1,0:T(8,128)}, f32[6,2,32,128]{3,2,1,0:T(8,128)S(1)}, u32[]{:S(2)}, u32[]{:S(2)}) collective-permute-start(f32[6,2,32,128]{3,2,1,0:T(8,128)} %get-tuple-element.127), channel_id=1, source_target_pairs={{0,128},{8,136},{16,144},{24,152},{32,160},{40,168},{48,176},{56,1... | collective-permute-start | bytes 589832 | tf_op jit(solution)/shard_map/ppermute | solution.py:368
  16.2 0.1 collective-permute-start.2
  16.3 0.6 %or_reduce_fusion = pred[]{:T(512)} fusion(s32[32,2]{0,1:T(2,128)S(1)} %slice_bitcast_fusion), kind=kLoop, calls=%fused_computation.5 | loop fusion | flops 767 | bytes 257 | tf_op jit(solution)/shard_map/reduce_and | solution.py:377
  17.5 6.5 %all-to-all-done.got = f32[8,10,32,128]{3,2,1,0:T(8,128)S(1)} async-done(((f32[8,10,32,128]{3,2,1,0:T(8,128)}), f32[8,10,32,128]{3,2,1,0:T(8,128)S(1)}, u32[]{:S(2)}, u32[]{:S(2)}) %all-to-all-start) | async-done | bytes 1310752 | tf_op jit(solution)/shard_map/all_to_all | solution.py:350
  24.1 1.2 %spectral.1 = f32[8,10,32,128]{3,2,1,0:T(8,128)} custom-call(f32[8,10,32,128]{3,2,1,0:T(8,128)S(1)} %all-to-all-done.got), custom_call_target="tpu_custom_call" | custom-call | flops 5242880 | bytes 2621440 | tf_op jit(solution)/shard_map/spectral/pallas_call | solution.py:392
  25.2 6.3 %all-to-all-start.1 = ((f32[8,10,32,128]{3,2,1,0:T(8,128)}), f32[8,10,32,128]{3,2,1,0:T(8,128)}, u32[]{:S(2)}, u32[]{:S(2)}) async-start(f32[8,10,32,128]{3,2,1,0:T(8,128)} %spectral.1), calls=%async_computation.1 | async-start | bytes 2621440 | tf_op jit(solution)/shard_map/all_to_all | solution.py:404
  31.6 0.0 collective-permute-done.1.half_hbm
  31.6 0.0 copy-done.10
  31.6 0.0 copy-start.7
  31.6 0.7 %copy-done.7 = f32[6,2,32,128]{3,2,1,0:T(8,128)} copy-done((f32[6,2,32,128]{3,2,1,0:T(8,128)}, f32[6,2,32,128]{3,2,1,0:T(8,128)S(1)}, u32[]{:S(2)}) %copy-start.7) | copy-done | bytes 196632
  32.2 0.0 collective-permute-done.2
  32.2 1.7 %factor.1 = f32[16,32,128]{2,1,0:T(8,128)} custom-call(f32[16,32,128]{2,1,0:T(8,128)} %vol.1, f32[16,32,128]{2,1,0:T(8,128)} %get-tuple-element.125.inv_dens.inv_hbm), custom_call_target="tpu_custom_call" | custom-call | tf_op jit(solution)/shard_map/factor/pallas_call | solution.py:406
  34.0 0.0 copy-start.2
  34.0 0.0 copy-start.3
  34.0 0.0 copy-start.4
  34.0 0.0 copy-start.5
  34.0 0.0 copy-start.8
  34.0 0.9 %copy-done.2 = f32[16,32,128]{2,1,0:T(8,128)S(1)} copy-done((f32[16,32,128]{2,1,0:T(8,128)S(1)}, f32[16,32,128]{2,1,0:T(8,128)}, u32[]{:S(2)}) %copy-start.2) | copy-done | bytes 262168
  34.9 0.1 copy-done.3
  35.0 0.0 copy-done.4
  35.0 0.0 copy-done.5
  35.0 0.1 copy-done.8
  35.1 0.0 copy-start
  35.1 1.3 %copy-done = f32[1,5,16,32,128]{4,3,2,1,0:T(8,128)S(1)} copy-done((f32[1,5,16,32,128]{4,3,2,1,0:T(8,128)S(1)}, f32[1,5,16,32,128]{4,3,2,1,0:T(8,128)}, u32[]{:S(2)}) %copy-start) | copy-done | bytes 1310744
  36.4 0.0 copy-start.6
  36.4 1.3 %copy-done.6 = f32[5,16,32,128]{3,2,1,0:T(8,128)S(1)} copy-done((f32[5,16,32,128]{3,2,1,0:T(8,128)S(1)}, f32[5,16,32,128]{3,2,1,0:T(8,128)}, u32[]{:S(2)}) %copy-start.6) | copy-done | bytes 1310744
  37.7 0.0 copy-start.1
  37.7 3.6 %circumferential.1.kept = f32[5,16,32,128]{3,2,1,0:T(8,128)S(1)} custom-call(s32[32,2,3]{2,1,0:T(2,128)S(1)} %copy-done.4, s32[32]{0:T(128)S(1)} %copy-done.5, f32[5,16,32,128]{3,2,1,0:T(8,128)S(1)} %bitcast.15, f32[16,32,128]{2,1,0:T(8,128)S(1)} %copy-done.3, f32[5,16,32,128]{3,2,1,0:T(8,128)S(1)} %copy-done.6, f32[16,32,128]{2,1,0:T(8,128)S(1)} %copy-done.2, ...), custom_call_target="tpu_custom_call" | custom-call | flops 65536000000 | bytes 3932160 | tf_op jit(solution)/shard_map/circumferential/pallas_call | solution.py:417
  41.4 5.9 %all-to-all-done.1 = f32[8,10,32,128]{3,2,1,0:T(8,128)} async-done(((f32[8,10,32,128]{3,2,1,0:T(8,128)}), f32[8,10,32,128]{3,2,1,0:T(8,128)}, u32[]{:S(2)}, u32[]{:S(2)}) %all-to-all-start.1) | async-done | bytes 1310752 | tf_op jit(solution)/shard_map/all_to_all | solution.py:404
  47.3 0.0 copy-done.1
  47.3 2.1 %final.1 = f32[5,16,32,128]{3,2,1,0:T(8,128)} custom-call(f32[5,16,32,128]{3,2,1,0:T(8,128)S(1)} %circumferential.1.kept, f32[16,32,128]{2,1,0:T(8,128)S(1)} %copy-done.1, f32[5,16,32,128]{3,2,1,0:T(8,128)} %bitcast.8.source_hbm), custom_call_target="tpu_custom_call" | custom-call | tf_op jit(solution)/shard_map/final/pallas_call | solution.py:430
  (2 shorter events, 0.0 us)
Async XLA Ops:
  0.0 6.1 %copy-start.9 = (s32[32,2,3]{0,1,2:T(2,128)S(1)}, s32[32,2,3]{0,1,2:T(2,128)}, u32[]{:S(2)}) copy-start(s32[32,2,3]{0,1,2:T(2,128)} %param.14) | copy-start | bytes 2308
  0.0 24.1 %all-to-all-start = ((f32[8,10,32,128]{3,2,1,0:T(8,128)}), f32[8,10,32,128]{3,2,1,0:T(8,128)S(1)}, u32[]{:S(2)}, u32[]{:S(2)}) async-start(f32[8,10,32,128]{3,2,1,0:T(8,128)} %bitcast.13), calls=%async_computation | async-start | bytes 2621440 | tf_op jit(solution)/shard_map/all_to_all | solution.py:350
  14.1 17.5 %copy-start.10 = (f32[6,2,32,128]{3,2,1,0:T(8,128)}, f32[6,2,32,128]{3,2,1,0:T(8,128)S(1)}, u32[]{:S(2)}) copy-start(f32[6,2,32,128]{3,2,1,0:T(8,128)S(1)} %get-tuple-element.128) | copy-start | bytes 589828
  14.1 17.5 %collective-permute-start.1 = (f32[6,2,32,128]{3,2,1,0:T(8,128)}, f32[6,2,32,128]{3,2,1,0:T(8,128)S(1)}, u32[]{:S(2)}, u32[]{:S(2)}) collective-permute-start(f32[6,2,32,128]{3,2,1,0:T(8,128)} %get-tuple-element.127), channel_id=1, source_target_pairs={{0,128},{8,136},{16,144},{24,152},{32,160},{40,168},{48,176},{56,1... | collective-permute-start | bytes 589832 | tf_op jit(solution)/shard_map/ppermute | solution.py:368
  16.2 16.0 %collective-permute-start.2 = (f32[6,2,32,128]{3,2,1,0:T(8,128)S(1)}, f32[6,2,32,128]{3,2,1,0:T(8,128)}, u32[]{:S(2)}, u32[]{:S(2)}) collective-permute-start(f32[6,2,32,128]{3,2,1,0:T(8,128)S(1)} %get-tuple-element.128), channel_id=1, source_target_pairs={{0,248},{8,128},{16,136},{24,144},{32,152},{40,160},{48,168},{56,1... | collective-permute-start | bytes 589832 | tf_op jit(solution)/shard_map/ppermute | solution.py:370
  25.2 22.0 %all-to-all-start.1 = ((f32[8,10,32,128]{3,2,1,0:T(8,128)}), f32[8,10,32,128]{3,2,1,0:T(8,128)}, u32[]{:S(2)}, u32[]{:S(2)}) async-start(f32[8,10,32,128]{3,2,1,0:T(8,128)} %spectral.1), calls=%async_computation.1 | async-start | bytes 2621440 | tf_op jit(solution)/shard_map/all_to_all | solution.py:404
  31.6 0.7 %copy-start.7 = (f32[6,2,32,128]{3,2,1,0:T(8,128)}, f32[6,2,32,128]{3,2,1,0:T(8,128)S(1)}, u32[]{:S(2)}) copy-start(f32[6,2,32,128]{3,2,1,0:T(8,128)S(1)} %collective-permute-done.1.half_hbm) | copy-start | bytes 589828
  34.0 0.9 %copy-start.2 = (f32[16,32,128]{2,1,0:T(8,128)S(1)}, f32[16,32,128]{2,1,0:T(8,128)}, u32[]{:S(2)}) copy-start(f32[16,32,128]{2,1,0:T(8,128)} %get-tuple-element.125.inv_dens.inv_hbm) | copy-start | bytes 786436
  34.0 1.0 %copy-start.3 = (f32[16,32,128]{2,1,0:T(8,128)S(1)}, f32[16,32,128]{2,1,0:T(8,128)}, u32[]{:S(2)}) copy-start(f32[16,32,128]{2,1,0:T(8,128)} %visc.1) | copy-start | bytes 786436
  34.0 1.0 %copy-start.4 = (s32[32,2,3]{2,1,0:T(2,128)S(1)}, s32[32,2,3]{2,1,0:T(2,128)}, u32[]{:S(2)}) copy-start(s32[32,2,3]{2,1,0:T(2,128)} %copy.8.connect) | copy-start | bytes 2308
  34.0 1.0 %copy-start.5 = (s32[32]{0:T(128)S(1)}, s32[32]{0:T(128)}, u32[]{:S(2)}) copy-start(s32[32]{0:T(128)} %counts.3) | copy-start | bytes 388
  34.0 1.1 %copy-start.8 = (f32[6,2,32,128]{3,2,1,0:T(8,128)S(1)}, f32[6,2,32,128]{3,2,1,0:T(8,128)}, u32[]{:S(2)}) copy-start(f32[6,2,32,128]{3,2,1,0:T(8,128)} %copy-done.7) | copy-start | bytes 589828
  35.1 1.3 %copy-start = (f32[1,5,16,32,128]{4,3,2,1,0:T(8,128)S(1)}, f32[1,5,16,32,128]{4,3,2,1,0:T(8,128)}, u32[]{:S(2)}) copy-start(f32[1,5,16,32,128]{4,3,2,1,0:T(8,128)} %param.11) | copy-start | bytes 3932164
  36.4 1.3 %copy-start.6 = (f32[5,16,32,128]{3,2,1,0:T(8,128)S(1)}, f32[5,16,32,128]{3,2,1,0:T(8,128)}, u32[]{:S(2)}) copy-start(f32[5,16,32,128]{3,2,1,0:T(8,128)} %get-tuple-element.126.kept_hbm) | copy-start | bytes 3932164
  37.7 9.5 %copy-start.1 = (f32[16,32,128]{2,1,0:T(8,128)S(1)}, f32[16,32,128]{2,1,0:T(8,128)}, u32[]{:S(2)}) copy-start(f32[16,32,128]{2,1,0:T(8,128)} %factor.1) | copy-start | bytes 786436
